TPU v7x, 256 devices: a whole 4x4x8 slice. The times are simulated.
256 devices in a mesh: pair: 8 (over z_lo, y), win: 32 (over z_hi, x, core).
Axes of the slice: x: 4, y: 4, z: 8 (z_hi: 4, z_lo: 2; z = z_hi * 2 + z_lo), core: 2. Of those that a mesh axis runs over, the one named last changes fastest.
Arguments:
- spectra: bfloat16 [2, 256, 256, 5120], P(None, 'win', None, 'pair'), may hold values from -3000 to 3000
- plan: int32 [7, 8], replicated, may hold values from 0 to 15, as said below
- round_index: int32 [1], replicated, may hold values from 0 to 6
Outputs:
- cross_spectra: bfloat16 [2, 4, 256, 640, 640], P(None, None, ('pair', 'win'))
Inputs may be any that keep to these rules, and one draw needn't show every extreme that they name: `plan`: row r pairs the blocks: entry [r, q] mod 8 is the opponent of block q, the pairing is mutual, no block meets itself, over the 7 rows every block meets every other block once, and of each pair exactly one block has entry // 8 equal to 1.
All inputs are finite; a program needn't handle non-finite values.
Results may differ from a plain program's by a relative error of at most 0.0034.
Values may be sent and summed in bfloat16 or wider, within the bound.
No kernel may reach another device: no remote copies, remote signals or barrier semaphores. Data moves between devices by JAX's collectives and lax.ppermute only.
A program may use at most 64 MiB of HBM per device.

v0:
```python
import jax
import jax.numpy as jnp
from jax import lax
from jax.sharding import PartitionSpec as P

EPS = 1e-06


def whiten(spectra):
    real_part = spectra[0].astype(jnp.float32)
    imag_part = spectra[1].astype(jnp.float32)
    energy = jnp.mean(real_part * real_part + imag_part * imag_part, axis=1, keepdims=True)
    inverse = lax.rsqrt(energy + EPS)
    return jnp.stack([real_part * inverse, imag_part * inverse]).astype(jnp.bfloat16)


def pair_lists(plan, round_index):
    block_count = plan.shape[1]
    entries = jnp.take(plan, round_index, axis=0)[0]
    opponents = jnp.mod(entries, block_count)
    home_flag = entries // block_count
    ranking = jnp.argsort(jnp.where(home_flag == 1, 0, 1).astype(jnp.int32), stable=True)
    leaders = ranking[: block_count // 2]
    return (leaders, jnp.take(opponents, leaders))


def spectra_products(leading, trailing):
    real_sum = jnp.einsum(
        "wfqi,wfqj->fqij", leading[0], trailing[0], preferred_element_type=jnp.float32
    )
    real_sum = real_sum + jnp.einsum(
        "wfqi,wfqj->fqij", leading[1], trailing[1], preferred_element_type=jnp.float32
    )
    imag_sum = jnp.einsum(
        "wfqi,wfqj->fqij", leading[1], trailing[0], preferred_element_type=jnp.float32
    )
    imag_sum = imag_sum - jnp.einsum(
        "wfqi,wfqj->fqij", leading[0], trailing[1], preferred_element_type=jnp.float32
    )
    return jnp.stack([real_sum, imag_sum], axis=1)


def body(spectra, plan, round_index):
    pair_count = lax.axis_size("pair")
    win_count = lax.axis_size("win")
    windows = spectra.shape[1]
    bins_all = spectra.shape[2]
    block_width = spectra.shape[3]
    bins_dev = bins_all // (pair_count * win_count)
    whitened = whiten(spectra).reshape(2, windows, pair_count, win_count, bins_dev, block_width)
    leaders, partner = pair_lists(plan, round_index)
    window_count = windows * win_count
    arrived = lax.all_to_all(
        lax.all_to_all(whitened, "pair", split_axis=2, concat_axis=5, tiled=True),
        "win",
        split_axis=3,
        concat_axis=1,
        tiled=True,
    )
    spread = arrived.reshape(2, window_count, bins_dev, pair_count, block_width)
    leading = jnp.take(spread, leaders, axis=3)
    trailing = jnp.take(spread, partner, axis=3)
    stacked = spectra_products(leading, trailing)
    return (jnp.transpose(stacked, (1, 2, 0, 3, 4)) / window_count).astype(jnp.bfloat16)


def solution(mesh):
    placed = (P(None, "win", None, "pair"), P(), P())
    return jax.shard_map(
        body,
        mesh=mesh,
        in_specs=placed,
        out_specs=P(None, None, ("pair", "win"), None, None),
        check_vma=False,
    )
```

profile of v0, /device:TPU:1, one launch (start us, length us, event | category | flops | bytes accessed | tf_op | source)
XLA Modules:
  0.0 264.7 jit_solution(14143076396766606725)
XLA Ops:
  0.0 0.0 copy-start
  0.0 3.7 %fusion.3 = f32[8,640]{1,0:T(8,128)S(1)} fusion(bf16[2,8,256,640]{3,2,1,0:T(8,128)(2,1)} %param.5), kind=kLoop, calls=%fused_computation.13 | loop fusion | flops 7859200 | bytes 5263360 | tf_op jit(solution)/shard_map/reduce_sum | solution.py:12
  3.8 0.3 copy-done
  4.1 1.2 fusion.4
  5.3 0.5 pad_maximum_fusion
  5.8 0.7 copy.22
  6.6 66.0 %all_to_all.33 = bf16[2,8,8,32,1,640]{5,3,1,0,4,2:T(8,128)(2,1)S(1)} all-to-all(bf16[2,8,8,32,1,640]{5,3,1,0,4,2:T(8,128)(2,1)S(1)} %copy.22), channel_id=1, replica_groups=mesh['pair'=8,'win'=32] {'pair'}, dimensions={2} | all-to-all | bytes 10485760 | tf_op jit(solution)/shard_map/all_to_all | solution.py:54
  72.6 5.4 %copy.32 = bf16[2,8,1,32,1,8,640]{6,5,1,0,3,4,2:T(8,128)(2,1)} copy(bf16[2,8,1,32,1,8,640]{6,3,1,0,5,4,2:T(8,128)(2,1)S(1)} %bitcast.66) | data formatting | bytes 10485760 | tf_op jit(solution)/shard_map/all_to_all | solution.py:54
  78.0 8.7 %reshape.197 = bf16[2,8,1,32,1,5120]{5,1,0,4,2,3:T(8,128)(2,1)} reshape(bf16[2,8,1,32,1,8,640]{6,5,1,0,3,4,2:T(8,128)(2,1)} %copy.32) | data formatting | bytes 10485760 | tf_op jit(solution)/shard_map/all_to_all | solution.py:54
  86.7 12.7 %all-to-all-start.1 = ((bf16[2,8,1,32,1,5120]{5,1,0,4,2,3:T(8,128)(2,1)}), bf16[2,8,1,32,1,5120]{5,1,0,4,2,3:T(8,128)(2,1)}, u32[]{:S(2)}, u32[]{:S(2)}) async-start(bf16[2,8,1,32,1,5120]{5,1,0,4,2,3:T(8,128)(2,1)} %reshape.197), calls=%async_computation.1 | async-start | bytes 10485760 | tf_op jit(solution)/shard_map/all_to_all | solution.py:53
  100.1 0.7 compare_select_fusion.2
  100.8 1.0 sort.17
  101.8 0.6 gather_fusion
  102.5 115.3 %all-to-all-done.1 = bf16[2,8,1,32,1,5120]{5,1,0,4,2,3:T(8,128)(2,1)} async-done(((bf16[2,8,1,32,1,5120]{5,1,0,4,2,3:T(8,128)(2,1)}), bf16[2,8,1,32,1,5120]{5,1,0,4,2,3:T(8,128)(2,1)}, u32[]{:S(2)}, u32[]{:S(2)}) %all-to-all-start.1) | async-done | bytes 5242912 | tf_op jit(solution)/shard_map/all_to_all | solution.py:53
  217.8 5.4 %copy.39 = bf16[2,8,1,32,1,5120]{5,3,1,0,4,2:T(8,128)(2,1)S(1)} copy(bf16[2,8,1,32,1,5120]{5,1,0,4,2,3:T(8,128)(2,1)} %all-to-all-done.1) | data formatting | bytes 10485760 | tf_op jit(solution)/shard_map/all_to_all | solution.py:53
  223.2 2.9 %copy.26 = bf16[2,32,8,1,1,1,5120]{6,2,1,0,5,4,3:T(8,128)(2,1)S(1)} copy(bf16[2,32,8,1,1,1,5120]{6,1,2,0,5,4,3:T(8,128)(2,1)S(1)} %bitcast.67) | data formatting | bytes 10485760 | tf_op jit(solution)/shard_map/all_to_all | solution.py:53
  226.0 1.2 copy.34
  227.2 3.2 %copy.38 = bf16[2,256,1,8,640]{4,1,3,0,2:T(8,128)(2,1)} copy(bf16[2,256,1,8,640]{4,3,1,0,2:T(8,128)(2,1)S(1)} %bitcast.69) | data formatting | bytes 10485760 | tf_op jit(solution)/shard_map/reshape | solution.py:60
  230.4 4.9 %gather_fusion.1 = bf16[4,2,256,640]{3,2,1,0:T(8,128)(2,1)} fusion(bf16[2,256,8,640]{3,1,2,0:T(8,128)(2,1)} %bitcast.70, s32[1024]{0:T(1024)S(1)} %pad_clamp_fusion.1), kind=kCustom, calls=%fused_computation.clone | custom fusion | bytes 5242896 | tf_op jit(solution)/shard_map/jit(_take)/gather | solution.py:61
  235.3 4.9 %gather_fusion.2 = bf16[4,2,256,640]{3,2,1,0:T(8,128)(2,1)} fusion(bf16[2,256,8,640]{3,1,2,0:T(8,128)(2,1)} %bitcast.71, s32[1024]{0:T(1024)S(1)} %pad_clamp_fusion), kind=kCustom, calls=%fused_computation.1.clone | custom fusion | bytes 5242896 | tf_op jit(solution)/shard_map/jit(_take)/gather | solution.py:62
  240.2 3.2 %copy.28 = bf16[4,2,256,640]{2,3,0,1:T(8,128)(2,1)S(1)} copy(bf16[4,2,256,640]{3,2,1,0:T(8,128)(2,1)} %gather_fusion.1) | data formatting | bytes 5242880 | tf_op jit(solution)/shard_map/jit(_take)/gather | solution.py:61
  243.4 2.1 bitcast_select_fusion
  245.5 0.3 bitcast_select_fusion.1
  245.8 1.2 fusion.7
  247.0 1.2 fusion.6
  248.2 3.9 %subtract_bitcast_fusion = f32[1,1,4,640,640]{4,3,2,1,0:T(8,128)} fusion(f32[4,640,640]{2,1,0:T(8,128)S(1)} %fusion.7, bf16[2,256,1,4,640]{1,4,3,2,0:T(8,128)(2,1)S(1)} %bitcast_select_fusion.1, bf16[2,256,1,4,640]{4,1,3,2,0:T(8,128)(2,1)S(1)} %bitcast_select_fusion), kind=kOutput, calls=%fused_computation.6 | convolution fusion | flops 840499200 | bytes 15728640 | tf_op jit(solution)/shard_map/wfqi,wfqj->fqij/dot_general | solution.py:37
  252.1 3.9 %add_bitcast_fusion = f32[1,1,4,640,640]{4,3,2,1,0:T(8,128)} fusion(f32[4,640,640]{2,1,0:T(8,128)S(1)} %fusion.6, bf16[2,256,1,4,640]{1,4,3,2,0:T(8,128)(2,1)S(1)} %bitcast_select_fusion.1, bf16[2,256,1,4,640]{4,1,3,2,0:T(8,128)(2,1)S(1)} %bitcast_select_fusion), kind=kOutput, calls=%fused_computation.7 | convolution fusion | flops 840499200 | bytes 15728640 | tf_op jit(solution)/shard_map/wfqi,wfqj->fqij/dot_general | solution.py:31
  256.0 8.7 %fusion.1 = bf16[2,4,1,640,640]{4,3,2,1,0:T(8,128)(2,1)} fusion(f32[1,1,4,640,640]{4,3,2,1,0:T(8,128)} %subtract_bitcast_fusion, f32[1,1,4,640,640]{4,3,2,1,0:T(8,128)} %add_bitcast_fusion), kind=kLoop, calls=%fused_computation.5 | loop fusion | flops 9830400 | bytes 19660800 | tf_op jit(solution)/shard_map/convert_element_type | solution.py:64
  (7 shorter events, 0.0 us)
Async XLA Ops:
  0.0 4.1 %copy-start = (bf16[2,8,256,640]{3,2,1,0:T(8,128)(2,1)S(1)}, bf16[2,8,256,640]{3,2,1,0:T(8,128)(2,1)}, u32[]{:S(2)}) copy-start(bf16[2,8,256,640]{3,2,1,0:T(8,128)(2,1)} %param.5) | copy-start | bytes 15728644
  86.7 131.1 %all-to-all-start.1 = ((bf16[2,8,1,32,1,5120]{5,1,0,4,2,3:T(8,128)(2,1)}), bf16[2,8,1,32,1,5120]{5,1,0,4,2,3:T(8,128)(2,1)}, u32[]{:S(2)}, u32[]{:S(2)}) async-start(bf16[2,8,1,32,1,5120]{5,1,0,4,2,3:T(8,128)(2,1)} %reshape.197), calls=%async_computation.1 | async-start | bytes 10485760 | tf_op jit(solution)/shard_map/all_to_all | solution.py:53
where the time goes:
time: 265 us
  waiting for transfers between devices  115 us (43%)
  blocking collectives  66 us (25%)
  local copies, waits for them, and re-layouts  41.4 us (16%)
  other arithmetic  18.3 us (7%)
  starting transfers between devices  12.7 us (5%)
  matrix products  10.2 us (4%)
    all_to_all x1, waiting for transfers between devices, body(): lax.all_to_all(lax.all_to_all(whitened, 'pair', split_axis=2, concat_axis...  115 us
    all_to_all x1, blocking collectives, body(): lax.all_to_all(whitened, 'pair', split_axis=2, concat_axis=5, tiled=True)  66 us
    all_to_all x2, local copies, waits for them, and re-layouts, body(): lax.all_to_all(whitened, 'pair', split_axis=2, concat_axis=5, tiled=True)  14.1 us
    all_to_all x1, starting transfers between devices, body(): lax.all_to_all(lax.all_to_all(whitened, 'pair', split_axis=2, concat_axis...  12.7 us
    convert_element_type x1, other arithmetic, body(): (jnp.transpose(stacked, (1, 2, 0, 3, 4)) / window_count).astype(jnp.bfloa...  8.74 us
    all_to_all x2, local copies, waits for them, and re-layouts, body(): lax.all_to_all(lax.all_to_all(whitened, 'pair', split_axis=2, concat_axis...  8.23 us
    gather x2, local copies, waits for them, and re-layouts, body(): leading = jnp.take(spread, leaders, axis=3)  8.09 us
  transfers between devices with their start and end apart: 1, of which 1 were waited for; matrix products, arithmetic and copies ran while one was open for 1% of the time, Pallas kernels for 0%

commit v1 on v0

v1 whole, which is shorter than its diff:
```python
import jax
import jax.numpy as jnp
from jax import lax
from jax.experimental import pallas as pl
from jax.experimental.pallas import tpu as pltpu
from jax.sharding import PartitionSpec as P

EPS = 1e-06
LANES = 128


def whiten_kernel(x_ref, o_ref, scaled):
    _, windows, bins, _ = x_ref.shape
    for w in range(windows):
        real = x_ref[0, w].astype(jnp.float32)
        imag = x_ref[1, w].astype(jnp.float32)
        energy = jnp.mean(real * real + imag * imag, axis=0, keepdims=True)
        inverse = lax.rsqrt(energy + EPS)
        scaled[0, w * bins : (w + 1) * bins] = real * inverse
        scaled[1, w * bins : (w + 1) * bins] = imag * inverse
    for f in range(bins):
        rows = pl.ds(f, windows, stride=bins)
        o_ref[f] = jnp.concatenate([scaled[0, rows], scaled[1, rows]], axis=0).astype(o_ref.dtype)


def whiten(spectra):
    _, windows, bins, width = spectra.shape
    return pl.pallas_call(
        whiten_kernel,
        grid=(width // LANES,),
        in_specs=[pl.BlockSpec((2, windows, bins, LANES), lambda i: (0, 0, 0, i))],
        out_specs=pl.BlockSpec((bins, 2 * windows, LANES), lambda i: (0, 0, i)),
        out_shape=jax.ShapeDtypeStruct((bins, 2 * windows, width), jnp.bfloat16),
        scratch_shapes=[pltpu.VMEM((2, windows * bins, LANES), jnp.float32)],
        compiler_params=pltpu.CompilerParams(vmem_limit_bytes=48 * 1024 * 1024),
        name="whiten",
    )(spectra)


def leader_of(k, plan, round_index):
    row = round_index[0]
    seen = jnp.int32(0)
    leader = jnp.int32(0)
    for q in range(plan.shape[1]):
        home = plan[row, q] >> 3
        leader = leader + jnp.where(seen == k, home, 0) * q
        seen = seen + home
    return leader


def rival_of(k, plan, round_index):
    return plan[round_index[0], leader_of(k, plan, round_index)] & 7


def products_kernel(plan, round_index, lead_ref, trail_ref, o_ref):
    _, sources, parts, width = lead_ref.shape
    half = parts // 2
    rows = sources * parts
    lead = lead_ref[0].reshape(rows, width)
    trail = trail_ref[0]
    wide = trail.astype(jnp.float32)
    turned = jnp.concatenate([-wide[:, half:], wide[:, :half]], axis=1).astype(jnp.bfloat16)
    scale = 2.0 / rows
    for part, other in ((0, trail), (1, turned)):
        total = lax.dot_general(
            lead,
            other.reshape(rows, width),
            (((0,), (0,)), ((), ())),
            preferred_element_type=jnp.float32,
        )
        o_ref[part, 0] = (total * scale).astype(o_ref.dtype)


def products(arrived, plan, round_index):
    blocks, sources, parts, width = arrived.shape
    block = (1, sources, parts, width)
    return pl.pallas_call(
        products_kernel,
        grid_spec=pltpu.PrefetchScalarGridSpec(
            num_scalar_prefetch=2,
            grid=(blocks // 2,),
            in_specs=[
                pl.BlockSpec(block, lambda k, plan, ri: (leader_of(k, plan, ri), 0, 0, 0)),
                pl.BlockSpec(block, lambda k, plan, ri: (rival_of(k, plan, ri), 0, 0, 0)),
            ],
            out_specs=pl.BlockSpec((2, 1, width, width), lambda k, plan, ri: (0, k, 0, 0)),
        ),
        out_shape=jax.ShapeDtypeStruct((2, blocks // 2, width, width), jnp.bfloat16),
        compiler_params=pltpu.CompilerParams(vmem_limit_bytes=48 * 1024 * 1024),
        name="products",
    )(plan, round_index, arrived, arrived)


def body(spectra, plan, round_index):
    pair_count = lax.axis_size("pair")
    win_count = lax.axis_size("win")
    whitened = whiten(spectra)
    arrived = lax.all_to_all(whitened, ("pair", "win"), split_axis=0, concat_axis=0, tiled=True)
    arrived = arrived.reshape(pair_count, win_count, *arrived.shape[1:])
    return products(arrived, plan, round_index)[:, :, None]


def solution(mesh):
    placed = (P(None, "win", None, "pair"), P(), P())
    return jax.shard_map(
        body,
        mesh=mesh,
        in_specs=placed,
        out_specs=P(None, None, ("pair", "win"), None, None),
        check_vma=False,
    )
```

time: 265 us -> 156 us (0.59)
  blocking collectives: 66 us -> 0 us
  local copies, waits for them, and re-layouts: 41.4 us -> 2.36 us
  Pallas kernels: 0 us -> 18.5 us
  other arithmetic: 18.3 us -> 0 us
  matrix products: 10.2 us -> 0 us
  starting transfers between devices: 12.7 us -> 16.5 us
    all_to_all x1 -> x0, blocking collectives: 66 us -> none  [body(): lax.all_to_all(whitened, 'pair', split_axis=2, concat_axis=5, tiled=True)]
    all_to_all x4 -> x0, local copies, waits for them, and re-layouts: 22.3 us -> none  [the longest x2 14.1 us: body(): lax.all_to_all(whitened, 'pair', split_axis=2, concat_axis=5, tiled=True)]
    pallas_call x0 -> x2, Pallas kernels: none -> 18.5 us  [the longest x1 9.57 us: whiten(): pl.pallas_call(whiten_kernel, grid=(width // LANES,), in_specs=[pl.BlockS...]
    gather x4 -> x0, local copies, waits for them, and re-layouts: 13.6 us -> none  [the longest x2 8.09 us: body(): leading = jnp.take(spread, leaders, axis=3)]
    dot_general x4 -> x0, matrix products: 10.2 us -> none  [the longest x1 3.93 us: spectra_products(): jnp.einsum('wfqi,wfqj->fqij', leading[0], trailing[1], preferred_element_...]
    convert_element_type x1 -> x0, other arithmetic: 8.74 us -> none  [body(): (jnp.transpose(stacked, (1, 2, 0, 3, 4)) / window_count).astype(jnp.bfloa...]
    all_to_all x1, starting transfers between devices: 12.7 us -> 16.5 us  [body(): lax.all_to_all(whitened, ('pair', 'win'), split_axis=0, concat_axis=0, ti...]
    reduce_sum x1 -> x0, other arithmetic: 3.73 us -> none  [whiten(): jnp.mean(real_part * real_part + imag_part * imag_part, axis=1, keepdims=...]
  transfers between devices with their start and end apart: 1 -> 1, of which waited for: 1 -> 1; matrix products, arithmetic and copies ran while one was open for 1% -> 0% of each run, Pallas kernels for 0% -> 0%
where the time goes in v1:
time: 156 us
  waiting for transfers between devices  117 us (75%)
  Pallas kernels  18.5 us (12%)
  starting transfers between devices  16.5 us (11%)
  local copies, waits for them, and re-layouts  2.36 us (2%)
    all_to_all x1, waiting for transfers between devices, body(): lax.all_to_all(whitened, ('pair', 'win'), split_axis=0, concat_axis=0, ti...  117 us
    all_to_all x1, starting transfers between devices, body(): lax.all_to_all(whitened, ('pair', 'win'), split_axis=0, concat_axis=0, ti...  16.5 us
    pallas_call x1, Pallas kernels, whiten(): pl.pallas_call(whiten_kernel, grid=(width // LANES,), in_specs=[pl.BlockS...  9.57 us
    pallas_call x1, Pallas kernels, products(): pl.pallas_call(products_kernel, grid_spec=pltpu.PrefetchScalarGridSpec(nu...  8.96 us
  transfers between devices with their start and end apart: 1, of which 1 were waited for; matrix products, arithmetic and copies ran while one was open for 0% of the time, Pallas kernels for 0%

profile of v1, /device:TPU:1, one launch (start us, length us, event | category | flops | bytes accessed | tf_op | source)
XLA Modules:
  0.0 155.6 jit_solution(11524705659301800481)
XLA Ops:
  0.0 9.6 %whiten.1 = bf16[256,16,640]{2,1,0:T(8,128)(2,1)S(1)} custom-call(bf16[2,8,256,640]{3,2,1,0:T(8,128)(2,1)} %x_ref.1), custom_call_target="tpu_custom_call" | custom-call | tf_op jit(solution)/shard_map/whiten/pallas_call | solution.py:28
  9.6 0.0 copy-start
  9.6 2.3 %copy-done = bf16[256,16,640]{2,1,0:T(8,128)(2,1)} copy-done((bf16[256,16,640]{2,1,0:T(8,128)(2,1)}, bf16[256,16,640]{2,1,0:T(8,128)(2,1)S(1)}, u32[]{:S(2)}) %copy-start) | copy-done | bytes 5242904
  11.9 0.0 copy-start.1
  11.9 16.5 %all-to-all-start = ((bf16[256,16,640]{2,1,0:T(8,128)(2,1)}), bf16[256,16,640]{2,1,0:T(8,128)(2,1)}, u32[]{:S(2)}, u32[]{:S(2)}) async-start(bf16[256,16,640]{2,1,0:T(8,128)(2,1)} %copy-done), calls=%async_computation | async-start | bytes 10485760 | tf_op jit(solution)/shard_map/all_to_all | solution.py:98
  29.1 117.5 %all-to-all-done = bf16[256,16,640]{2,1,0:T(8,128)(2,1)} async-done(((bf16[256,16,640]{2,1,0:T(8,128)(2,1)}), bf16[256,16,640]{2,1,0:T(8,128)(2,1)}, u32[]{:S(2)}, u32[]{:S(2)}) %all-to-all-start) | async-done | bytes 5242912 | tf_op jit(solution)/shard_map/all_to_all | solution.py:98
  146.6 0.0 copy-done.1
  146.6 9.0 %products.1 = bf16[2,4,640,640]{3,2,1,0:T(8,128)(2,1)} custom-call(s32[7,8]{1,0:T(8,128)S(1)} %copy-done.1, s32[1]{0:T(128)S(6)} %copy.5.round_index, bf16[8,32,16,640]{3,2,1,0:T(8,128)(2,1)} %bitcast.lead_ref.trail_ref, bf16[8,32,16,640]{3,2,1,0:T(8,128)(2,1)} %bitcast.lead_ref.trail_ref), custom_call_target="tpu_custom_call" | custom-call | tf_op jit(solution)/shard_map/products/pallas_call | solution.py:77
Async XLA Ops:
  9.6 2.4 %copy-start = (bf16[256,16,640]{2,1,0:T(8,128)(2,1)}, bf16[256,16,640]{2,1,0:T(8,128)(2,1)S(1)}, u32[]{:S(2)}) copy-start(bf16[256,16,640]{2,1,0:T(8,128)(2,1)S(1)} %whiten.1) | copy-start | bytes 15728644
  11.9 134.7 %copy-start.1 = (s32[7,8]{1,0:T(8,128)S(1)}, s32[7,8]{1,0:T(8,128)}, u32[]{:S(2)}) copy-start(s32[7,8]{1,0:T(8,128)} %plan.1) | copy-start | bytes 676
  11.9 134.7 %all-to-all-start = ((bf16[256,16,640]{2,1,0:T(8,128)(2,1)}), bf16[256,16,640]{2,1,0:T(8,128)(2,1)}, u32[]{:S(2)}, u32[]{:S(2)}) async-start(bf16[256,16,640]{2,1,0:T(8,128)(2,1)} %copy-done), calls=%async_computation | async-start | bytes 10485760 | tf_op jit(solution)/shard_map/all_to_all | solution.py:98

commit v2 on v0

v2 whole, which is shorter than its diff:
```python
import jax
import jax.numpy as jnp
from jax import lax
from jax.experimental import pallas as pl
from jax.experimental.pallas import tpu as pltpu
from jax.sharding import PartitionSpec as P

EPS = 1e-06
LANES = 128
ROWS = 32
GROUP = 16
VMEM_LIMIT = 24 * 1024 * 1024


def list_pairs(plan, round_index, pairs):
    blocks = plan.shape[1]
    entries = [plan[round_index[0], q] for q in range(blocks)]
    for k in range(blocks // 2):
        seen = jnp.int32(0)
        leader = jnp.int32(0)
        rival = jnp.int32(0)
        for q, entry in enumerate(entries):
            home = entry >> 3
            hit = jnp.where(seen == k, home, 0)
            leader = leader + hit * q
            rival = rival + hit * (entry & 7)
            seen = seen + home
        pairs[0, k] = leader
        pairs[1, k] = rival


def whiten_kernel(plan_hbm, round_hbm, x_hbm, o_ref, pairs, x_vmem, scale, plan, round_index, sems, small_sems):
    _, windows, bins, width = x_hbm.shape

    def copy(w):
        return pltpu.make_async_copy(x_hbm.at[:, w], x_vmem.at[:, w], sems.at[w])

    small = (
        pltpu.make_async_copy(plan_hbm, plan, small_sems.at[0]),
        pltpu.make_async_copy(round_hbm, round_index, small_sems.at[1]),
    )
    for c in small:
        c.start()
    for w in range(windows):
        copy(w).start()

    series = 2 * windows
    count = series * GROUP
    row = lax.broadcasted_iota(jnp.int32, (count, count), 0)
    column = lax.broadcasted_iota(jnp.int32, (count, count), 1)
    source = lax.rem(row, series) * GROUP + lax.div(row, series)
    swap = jnp.where(column == source, 1.0, 0.0).astype(jnp.bfloat16)

    for c in small:
        c.wait()
    list_pairs(plan, round_index, pairs)

    def one_window(w, carry):
        copy(w).wait()
        energies = []
        for lane in range(0, width, LANES):
            lanes = slice(lane, lane + LANES)
            totals = [jnp.zeros((8, LANES), jnp.float32) for _ in range(4)]
            for f in range(0, bins, ROWS):
                for part in range(2):
                    v = x_vmem[part, w, f : f + ROWS, lanes].astype(jnp.float32)
                    v = (v * v).reshape(ROWS // 8, 8, LANES)
                    for r in range(ROWS // 8):
                        totals[r % 4] = totals[r % 4] + v[r]
            total = (totals[0] + totals[1]) + (totals[2] + totals[3])
            energies.append(jnp.sum(total, axis=0, keepdims=True))
        energy = jnp.concatenate(energies, axis=1) * (1.0 / bins)
        scale[pl.ds(w, 1)] = lax.rsqrt(energy + EPS)
        return carry

    lax.fori_loop(0, windows, one_window, 0)
    inverse = scale[...]

    def one_group(g, carry):
        rows = pl.ds(pl.multiple_of(g * GROUP, GROUP), GROUP)
        moved = jnp.dot(swap, x_vmem[:, :, rows, :].reshape(count, width), preferred_element_type=jnp.float32)
        whitened = moved.reshape(2 * GROUP, windows, width) * inverse
        o_ref[rows] = whitened.astype(o_ref.dtype).reshape(GROUP, series, width)
        return carry

    lax.fori_loop(0, bins // GROUP, one_group, 0, unroll=True)


def whiten(spectra, plan, round_index):
    _, windows, bins, width = spectra.shape
    hbm = pl.BlockSpec(memory_space=pltpu.HBM)
    plan = pltpu.with_memory_space_constraint(plan, pltpu.HBM)
    spectra = pltpu.with_memory_space_constraint(spectra, pltpu.HBM)
    return pl.pallas_call(
        whiten_kernel,
        in_specs=[hbm, hbm, hbm],
        out_specs=[pl.BlockSpec(memory_space=pltpu.VMEM), pl.BlockSpec(memory_space=pltpu.SMEM)],
        out_shape=[
            jax.ShapeDtypeStruct((bins, 2 * windows, width), jnp.bfloat16),
            jax.ShapeDtypeStruct((2, plan.shape[1] // 2), jnp.int32),
        ],
        scratch_shapes=[
            pltpu.VMEM((2, windows, bins, width), jnp.bfloat16),
            pltpu.VMEM((windows, width), jnp.float32),
            pltpu.SMEM(plan.shape, jnp.int32),
            pltpu.SMEM(round_index.shape, jnp.int32),
            pltpu.SemaphoreType.DMA((windows,)),
            pltpu.SemaphoreType.DMA((2,)),
        ],
        compiler_params=pltpu.CompilerParams(vmem_limit_bytes=VMEM_LIMIT),
        name="whiten",
    )(plan, round_index, spectra)


def products_kernel(pairs, a_ref, o_hbm, held, out_sems):
    blocks, sources, parts, width = a_ref.shape
    half = parts // 2
    rows = sources * parts
    scale = 2.0 / rows

    def sent(k, slot):
        return pltpu.make_async_copy(held.at[slot], o_hbm.at[:, k], out_sems.at[slot])

    for k in range(blocks // 2):
        lead = a_ref[pairs[0, k]].reshape(rows, width)
        trail = a_ref[pairs[1, k]]
        wide = trail.astype(jnp.float32)
        turned = jnp.concatenate([-wide[:, half:], wide[:, :half]], axis=1).astype(jnp.bfloat16)
        slot = k % 2
        if k >= 2:
            sent(k - 2, slot).wait()
        for part, other in ((0, trail), (1, turned)):
            total = lax.dot_general(
                lead,
                other.reshape(rows, width),
                (((0,), (0,)), ((), ())),
                preferred_element_type=jnp.float32,
            )
            held[slot, part] = (total * scale).astype(held.dtype)
        sent(k, slot).start()
    for k in range(blocks // 2 - 2, blocks // 2):
        sent(k, k % 2).wait()


def products(arrived, pairs):
    blocks, sources, parts, width = arrived.shape
    return pl.pallas_call(
        products_kernel,
        in_specs=[
            pl.BlockSpec(memory_space=pltpu.SMEM),
            pl.BlockSpec(memory_space=pltpu.VMEM),
        ],
        out_specs=pl.BlockSpec(memory_space=pl.ANY),
        out_shape=jax.ShapeDtypeStruct((2, blocks // 2, width, width), jnp.bfloat16),
        scratch_shapes=[
            pltpu.VMEM((2, 2, width, width), jnp.bfloat16),
            pltpu.SemaphoreType.DMA((2,)),
        ],
        compiler_params=pltpu.CompilerParams(vmem_limit_bytes=VMEM_LIMIT),
        name="products",
    )(pairs, arrived)


def body(spectra, plan, round_index):
    pair_count = lax.axis_size("pair")
    win_count = lax.axis_size("win")
    whitened, pairs = whiten(spectra, plan, round_index)
    arrived = lax.all_to_all(whitened, ("pair", "win"), split_axis=0, concat_axis=0, tiled=True)
    arrived = arrived.reshape(pair_count, win_count, *arrived.shape[1:])
    return products(arrived, pairs)[:, :, None]


def solution(mesh):
    placed = (P(None, "win", None, "pair"), P(), P())
    return jax.shard_map(
        body,
        mesh=mesh,
        in_specs=placed,
        out_specs=P(None, None, ("pair", "win"), None, None),
        check_vma=False,
    )
```

time: 265 us -> 146 us (0.55)
  waiting for transfers between devices: 115 us -> 0 us
  blocking collectives: 66 us -> 134 us
  local copies, waits for them, and re-layouts: 41.4 us -> 0 us
  other arithmetic: 18.3 us -> 0 us
  starting transfers between devices: 12.7 us -> 0 us
  Pallas kernels: 0 us -> 11.2 us
  matrix products: 10.2 us -> 0 us
    all_to_all x1 -> x0, waiting for transfers between devices: 115 us -> none  [body(): lax.all_to_all(lax.all_to_all(whitened, 'pair', split_axis=2, concat_axis...]
    all_to_all x1, blocking collectives: 66 us -> 134 us  [body(): lax.all_to_all(whitened, ('pair', 'win'), split_axis=0, concat_axis=0, ti...]
    all_to_all x4 -> x0, local copies, waits for them, and re-layouts: 22.3 us -> none  [the longest x2 14.1 us: body(): lax.all_to_all(whitened, 'pair', split_axis=2, concat_axis=5, tiled=True)]
    gather x4 -> x0, local copies, waits for them, and re-layouts: 13.6 us -> none  [the longest x2 8.09 us: body(): leading = jnp.take(spread, leaders, axis=3)]
    all_to_all x1 -> x0, starting transfers between devices: 12.7 us -> none  [body(): lax.all_to_all(lax.all_to_all(whitened, 'pair', split_axis=2, concat_axis...]
    pallas_call x0 -> x2, Pallas kernels: none -> 11.2 us  [the longest x1 6.71 us: products(): pl.pallas_call(products_kernel, in_specs=[pl.BlockSpec(memory_space=pltpu...]
    dot_general x4 -> x0, matrix products: 10.2 us -> none  [the longest x1 3.93 us: spectra_products(): jnp.einsum('wfqi,wfqj->fqij', leading[0], trailing[1], preferred_element_...]
    convert_element_type x1 -> x0, other arithmetic: 8.74 us -> none  [body(): (jnp.transpose(stacked, (1, 2, 0, 3, 4)) / window_count).astype(jnp.bfloa...]
  transfers between devices with their start and end apart: 1 -> 0, of which waited for: 1 -> 0; matrix products, arithmetic and copies ran while one was open for 1% -> 0% of each run, Pallas kernels for 0% -> 0%
where the time goes in v2:
time: 146 us
  blocking collectives  134 us (92%)
  Pallas kernels  11.2 us (8%)
    all_to_all x1, blocking collectives, body(): lax.all_to_all(whitened, ('pair', 'win'), split_axis=0, concat_axis=0, ti...  134 us
    pallas_call x1, Pallas kernels, products(): pl.pallas_call(products_kernel, in_specs=[pl.BlockSpec(memory_space=pltpu...  6.71 us
    pallas_call x1, Pallas kernels, whiten(): pl.pallas_call(whiten_kernel, in_specs=[hbm, hbm, hbm], out_specs=[pl.Blo...  4.51 us

profile of v2, /device:TPU:1, one launch (start us, length us, event | category | flops | bytes accessed | tf_op | source)
XLA Modules:
  0.0 146.2 jit_solution(13909865083882805081)
XLA Ops:
  0.7 4.5 %whiten.1 = (bf16[256,16,640]{2,1,0:T(8,128)(2,1)S(1)}, s32[2,4]{1,0:T(2,128)S(1)}) custom-call(s32[7,8]{1,0:T(8,128)} %plan_hbm.1, s32[1]{0:T(128)S(6)} %copy.5.round_hbm, bf16[2,8,256,640]{3,2,1,0:T(8,128)(2,1)} %x_hbm.1), custom_call_target="tpu_custom_call" | custom-call | tf_op jit(solution)/shard_map/whiten/pallas_call | solution.py:94
  5.2 134.4 %all_to_all.5 = bf16[256,16,640]{2,1,0:T(8,128)(2,1)S(1)} all-to-all(bf16[256,16,640]{2,1,0:T(8,128)(2,1)S(1)} %get-tuple-element.8), channel_id=1, replica_groups=mesh['pair'=8,'win'=32] {'pair','win'}, dimensions={0} | all-to-all | bytes 10485760 | tf_op jit(solution)/shard_map/all_to_all | solution.py:168
  139.5 6.7 %products.1 = bf16[2,4,640,640]{3,2,1,0:T(8,128)(2,1)} custom-call(s32[2,4]{1,0:T(2,128)S(1)} %get-tuple-element.7.pairs, bf16[8,32,16,640]{3,2,1,0:T(8,128)(2,1)S(1)} %bitcast.4), custom_call_target="tpu_custom_call" | custom-call | tf_op jit(solution)/shard_map/products/pallas_call | solution.py:147

commit v3 on v2

--- a/solution.py
+++ b/solution.py
@@ -9,6 +9,7 @@
 LANES = 128
 ROWS = 32
 GROUP = 16
+TILE = 256
 VMEM_LIMIT = 24 * 1024 * 1024
 
 
@@ -112,34 +113,41 @@
     )(plan, round_index, spectra)
 
 
-def products_kernel(pairs, a_ref, o_hbm, held, out_sems):
+def products_kernel(pairs, a_ref, o_hbm, held, sems):
     blocks, sources, parts, width = a_ref.shape
     half = parts // 2
     rows = sources * parts
     scale = 2.0 / rows
 
-    def sent(k, slot):
-        return pltpu.make_async_copy(held.at[slot], o_hbm.at[:, k], out_sems.at[slot])
+    def sent(k, part):
+        return pltpu.make_async_copy(held.at[part, k], o_hbm.at[part, k], sems.at[part, k])
 
     for k in range(blocks // 2):
         lead = a_ref[pairs[0, k]].reshape(rows, width)
         trail = a_ref[pairs[1, k]]
         wide = trail.astype(jnp.float32)
         turned = jnp.concatenate([-wide[:, half:], wide[:, :half]], axis=1).astype(jnp.bfloat16)
-        slot = k % 2
-        if k >= 2:
-            sent(k - 2, slot).wait()
-        for part, other in ((0, trail), (1, turned)):
+        both = jnp.concatenate([trail.reshape(rows, width), turned.reshape(rows, width)], axis=1)
+        for first in range(0, 2 * width, TILE):
             total = lax.dot_general(
                 lead,
-                other.reshape(rows, width),
+                both[:, first : first + TILE],
                 (((0,), (0,)), ((), ())),
                 preferred_element_type=jnp.float32,
             )
-            held[slot, part] = (total * scale).astype(held.dtype)
-        sent(k, slot).start()
-    for k in range(blocks // 2 - 2, blocks // 2):
-        sent(k, k % 2).wait()
+            result = (total * scale).astype(held.dtype)
+            last = first + result.shape[1]
+            cut = min(max(width - first, 0), result.shape[1])
+            if cut:
+                held[0, k, :, first : first + cut] = result[:, :cut]
+            if cut < result.shape[1]:
+                held[1, k, :, first + cut - width : last - width] = result[:, cut:]
+            if first < width <= last:
+                sent(k, 0).start()
+        sent(k, 1).start()
+    for k in range(blocks // 2):
+        for part in range(2):
+            sent(k, part).wait()
 
 
 def products(arrived, pairs):
@@ -153,8 +161,8 @@
         out_specs=pl.BlockSpec(memory_space=pl.ANY),
         out_shape=jax.ShapeDtypeStruct((2, blocks // 2, width, width), jnp.bfloat16),
         scratch_shapes=[
-            pltpu.VMEM((2, 2, width, width), jnp.bfloat16),
-            pltpu.SemaphoreType.DMA((2,)),
+            pltpu.VMEM((2, blocks // 2, width, width), jnp.bfloat16),
+            pltpu.SemaphoreType.DMA((2, blocks // 2)),
         ],
         compiler_params=pltpu.CompilerParams(vmem_limit_bytes=VMEM_LIMIT),
         name="products",

time: 146 us -> 145 us (level)
  Pallas kernels: 11.2 us -> 9.73 us
    pallas_call x1, Pallas kernels: 6.71 us -> 5.22 us  [products(): pl.pallas_call(products_kernel, in_specs=[pl.BlockSpec(memory_space=pltpu...]
where the time goes in v3:
time: 145 us
  blocking collectives  134 us (92%)
  Pallas kernels  9.73 us (7%)
    all_to_all x1, blocking collectives, body(): lax.all_to_all(whitened, ('pair', 'win'), split_axis=0, concat_axis=0, ti...  134 us
    pallas_call x1, Pallas kernels, products(): pl.pallas_call(products_kernel, in_specs=[pl.BlockSpec(memory_space=pltpu...  5.22 us
    pallas_call x1, Pallas kernels, whiten(): pl.pallas_call(whiten_kernel, in_specs=[hbm, hbm, hbm], out_specs=[pl.Blo...  4.51 us

profile of v3, /device:TPU:1, one launch (start us, length us, event | category | flops | bytes accessed | tf_op | source)
XLA Modules:
  0.0 144.7 jit_solution(2597332328554497533)
XLA Ops:
  0.7 4.5 %whiten.1 = (bf16[256,16,640]{2,1,0:T(8,128)(2,1)S(1)}, s32[2,4]{1,0:T(2,128)S(1)}) custom-call(s32[7,8]{1,0:T(8,128)} %plan_hbm.1, s32[1]{0:T(128)S(6)} %copy.5.round_hbm, bf16[2,8,256,640]{3,2,1,0:T(8,128)(2,1)} %x_hbm.1), custom_call_target="tpu_custom_call" | custom-call | tf_op jit(solution)/shard_map/whiten/pallas_call | solution.py:95
  5.2 134.4 %all_to_all.5 = bf16[256,16,640]{2,1,0:T(8,128)(2,1)S(1)} all-to-all(bf16[256,16,640]{2,1,0:T(8,128)(2,1)S(1)} %get-tuple-element.8), channel_id=1, replica_groups=mesh['pair'=8,'win'=32] {'pair','win'}, dimensions={0} | all-to-all | bytes 10485760 | tf_op jit(solution)/shard_map/all_to_all | solution.py:176
  139.5 5.2 %products.1 = bf16[2,4,640,640]{3,2,1,0:T(8,128)(2,1)} custom-call(s32[2,4]{1,0:T(2,128)S(1)} %get-tuple-element.7.pairs, bf16[8,32,16,640]{3,2,1,0:T(8,128)(2,1)S(1)} %bitcast.4), custom_call_target="tpu_custom_call" | custom-call | tf_op jit(solution)/shard_map/products/pallas_call | solution.py:155

commit v4 on v3

--- a/solution.py
+++ b/solution.py
@@ -10,7 +10,15 @@
 ROWS = 32
 GROUP = 16
 TILE = 256
+JOIN = 2
+Z, Y, X, C = 8, 4, 4, 2
 VMEM_LIMIT = 24 * 1024 * 1024
+
+
+def slot_of(owner):
+    pair, win = divmod(owner, Z // 2 * X * C)
+    z, y, x, c = 2 * (win // (X * C)) + pair // Y, pair % Y, (win // C) % X, win % C
+    return ((c * X + x) * Y + y) * Z + z
 
 
 def list_pairs(plan, round_index, pairs):
@@ -77,14 +85,15 @@
     lax.fori_loop(0, windows, one_window, 0)
     inverse = scale[...]
 
-    def one_group(g, carry):
-        rows = pl.ds(pl.multiple_of(g * GROUP, GROUP), GROUP)
-        moved = jnp.dot(swap, x_vmem[:, :, rows, :].reshape(count, width), preferred_element_type=jnp.float32)
-        whitened = moved.reshape(2 * GROUP, windows, width) * inverse
-        o_ref[rows] = whitened.astype(o_ref.dtype).reshape(GROUP, series, width)
-        return carry
-
-    lax.fori_loop(0, bins // GROUP, one_group, 0, unroll=True)
+    for first in range(0, bins, JOIN * GROUP):
+        groups = range(first, first + JOIN * GROUP, GROUP)
+        rows = [x_vmem[:, :, f : f + GROUP].reshape(count, width) for f in groups]
+        moved = jnp.dot(swap, jnp.concatenate(rows, axis=1), preferred_element_type=jnp.float32)
+        for j, f in enumerate(groups):
+            group = moved[:, j * width : (j + 1) * width].reshape(2 * GROUP, windows, width) * inverse
+            group = group.astype(o_ref.dtype).reshape(GROUP, series, width)
+            for i in range(GROUP):
+                o_ref[slot_of(f + i)] = group[i]
 
 
 def whiten(spectra, plan, round_index):
@@ -114,17 +123,18 @@
 
 
 def products_kernel(pairs, a_ref, o_hbm, held, sems):
-    blocks, sources, parts, width = a_ref.shape
+    pieces, ys, highs, lows, parts, width = a_ref.shape
+    blocks = lows * ys
     half = parts // 2
-    rows = sources * parts
+    rows = pieces * highs * parts
     scale = 2.0 / rows
 
     def sent(k, part):
         return pltpu.make_async_copy(held.at[part, k], o_hbm.at[part, k], sems.at[part, k])
 
     for k in range(blocks // 2):
-        lead = a_ref[pairs[0, k]].reshape(rows, width)
-        trail = a_ref[pairs[1, k]]
+        lead = a_ref[:, pairs[0, k] & (Y - 1), :, pairs[0, k] >> 2].reshape(rows, width)
+        trail = a_ref[:, pairs[1, k] & (Y - 1), :, pairs[1, k] >> 2].reshape(pieces * highs, parts, width)
         wide = trail.astype(jnp.float32)
         turned = jnp.concatenate([-wide[:, half:], wide[:, :half]], axis=1).astype(jnp.bfloat16)
         both = jnp.concatenate([trail.reshape(rows, width), turned.reshape(rows, width)], axis=1)
@@ -151,7 +161,8 @@
 
 
 def products(arrived, pairs):
-    blocks, sources, parts, width = arrived.shape
+    *_, width = arrived.shape
+    blocks = 2 * Y
     return pl.pallas_call(
         products_kernel,
         in_specs=[
@@ -173,8 +184,11 @@
     pair_count = lax.axis_size("pair")
     win_count = lax.axis_size("win")
     whitened, pairs = whiten(spectra, plan, round_index)
-    arrived = lax.all_to_all(whitened, ("pair", "win"), split_axis=0, concat_axis=0, tiled=True)
-    arrived = arrived.reshape(pair_count, win_count, *arrived.shape[1:])
+    order = sorted(range(pair_count * win_count), key=slot_of)
+    arrived = lax.all_to_all(
+        whitened, ("pair", "win"), split_axis=0, concat_axis=0, tiled=True, axis_index_groups=[order]
+    )
+    arrived = arrived.reshape(C * X, Y, Z // 2, 2, *arrived.shape[1:])
     return products(arrived, pairs)[:, :, None]
 
 

time: 145 us -> 144 us (level)
  no operation moved by 1% of the time
where the time goes in v4:
time: 144 us
  blocking collectives  134 us (93%)
  Pallas kernels  9.46 us (7%)
    all_to_all x1, blocking collectives, body(): lax.all_to_all(whitened, ('pair', 'win'), split_axis=0, concat_axis=0, ti...  134 us
    pallas_call x1, Pallas kernels, products(): pl.pallas_call(products_kernel, in_specs=[pl.BlockSpec(memory_space=pltpu...  5.23 us
    pallas_call x1, Pallas kernels, whiten(): pl.pallas_call(whiten_kernel, in_specs=[hbm, hbm, hbm], out_specs=[pl.Blo...  4.24 us

profile of v4, /device:TPU:1, one launch (start us, length us, event | category | flops | bytes accessed | tf_op | source)
XLA Modules:
  0.0 144.0 jit_solution(1292169704750791110)
XLA Ops:
  0.7 4.2 %whiten.1 = (bf16[256,16,640]{2,1,0:T(8,128)(2,1)S(1)}, s32[2,4]{1,0:T(2,128)S(1)}) custom-call(s32[7,8]{1,0:T(8,128)} %plan_hbm.1, s32[1]{0:T(128)S(6)} %copy.5.round_hbm, bf16[2,8,256,640]{3,2,1,0:T(8,128)(2,1)} %x_hbm.1), custom_call_target="tpu_custom_call" | custom-call | tf_op jit(solution)/shard_map/whiten/pallas_call | solution.py:104
  4.9 133.8 %all_to_all.5 = bf16[256,16,640]{2,1,0:T(8,128)(2,1)S(1)} all-to-all(bf16[256,16,640]{2,1,0:T(8,128)(2,1)S(1)} %get-tuple-element.8), channel_id=1, replica_groups={{0,128,8,136,16,144,24,152,32,160,40,168,48,176,56,184,64,192,72,200,80..., dimensions={0} | all-to-all | bytes 10485760 | tf_op jit(solution)/shard_map/all_to_all | solution.py:188
  138.7 5.2 %products.1 = bf16[2,4,640,640]{3,2,1,0:T(8,128)(2,1)} custom-call(s32[2,4]{1,0:T(2,128)S(1)} %get-tuple-element.7.pairs, bf16[8,4,4,2,16,640]{5,4,3,2,1,0:T(8,128)(2,1)S(1)} %bitcast.4), custom_call_target="tpu_custom_call" | custom-call | tf_op jit(solution)/shard_map/products/pallas_call | solution.py:166

commit v5 on v4

--- a/solution.py
+++ b/solution.py
@@ -38,7 +38,9 @@
         pairs[1, k] = rival
 
 
-def whiten_kernel(plan_hbm, round_hbm, x_hbm, o_ref, pairs, x_vmem, scale, plan, round_index, sems, small_sems):
+def whiten_kernel(
+    plan_hbm, round_hbm, x_hbm, o_ref, pairs, x_vmem, early, scale, plan, round_index, sems, small_sems
+):
     _, windows, bins, width = x_hbm.shape
 
     def copy(w):
@@ -53,7 +55,8 @@
     for w in range(windows):
         copy(w).start()
 
-    series = 2 * windows
+    half = windows // 2
+    series = 2 * half
     count = series * GROUP
     row = lax.broadcasted_iota(jnp.int32, (count, count), 0)
     column = lax.broadcasted_iota(jnp.int32, (count, count), 1)
@@ -79,21 +82,27 @@
             total = (totals[0] + totals[1]) + (totals[2] + totals[3])
             energies.append(jnp.sum(total, axis=0, keepdims=True))
         energy = jnp.concatenate(energies, axis=1) * (1.0 / bins)
-        scale[pl.ds(w, 1)] = lax.rsqrt(energy + EPS)
+        inverse = lax.rsqrt(energy + EPS)
+        side = w // half
+        for part in range(2):
+            scale[side, pl.ds(part * half + w - side * half, 1)] = inverse
         return carry
 
-    lax.fori_loop(0, windows, one_window, 0)
-    inverse = scale[...]
-
-    for first in range(0, bins, JOIN * GROUP):
-        groups = range(first, first + JOIN * GROUP, GROUP)
-        rows = [x_vmem[:, :, f : f + GROUP].reshape(count, width) for f in groups]
-        moved = jnp.dot(swap, jnp.concatenate(rows, axis=1), preferred_element_type=jnp.float32)
-        for j, f in enumerate(groups):
-            group = moved[:, j * width : (j + 1) * width].reshape(2 * GROUP, windows, width) * inverse
-            group = group.astype(o_ref.dtype).reshape(GROUP, series, width)
-            for i in range(GROUP):
-                o_ref[slot_of(f + i)] = group[i]
+    for side in range(2):
+        lax.fori_loop(side * half, (side + 1) * half, one_window, 0)
+        inverse = scale[side]
+        for first in range(0, bins, JOIN * GROUP):
+            groups = range(first, first + JOIN * GROUP, GROUP)
+            rows = [x_vmem[:, side * half : (side + 1) * half, f : f + GROUP].reshape(count, width) for f in groups]
+            moved = jnp.dot(swap, jnp.concatenate(rows, axis=1), preferred_element_type=jnp.float32)
+            for j, f in enumerate(groups):
+                group = moved[:, j * width : (j + 1) * width].reshape(GROUP, series, width) * inverse
+                if side == 0:
+                    early[f : f + GROUP] = group
+                    continue
+                group = jnp.concatenate([early[f : f + GROUP], group], axis=1).astype(o_ref.dtype)
+                for i in range(GROUP):
+                    o_ref[slot_of(f + i)] = group[i]
 
 
 def whiten(spectra, plan, round_index):
@@ -111,7 +120,8 @@
         ],
         scratch_shapes=[
             pltpu.VMEM((2, windows, bins, width), jnp.bfloat16),
-            pltpu.VMEM((windows, width), jnp.float32),
+            pltpu.VMEM((bins, windows, width), jnp.float32),
+            pltpu.VMEM((2, windows, width), jnp.float32),
             pltpu.SMEM(plan.shape, jnp.int32),
             pltpu.SMEM(round_index.shape, jnp.int32),
             pltpu.SemaphoreType.DMA((windows,)),
@@ -125,18 +135,20 @@
 def products_kernel(pairs, a_ref, o_hbm, held, sems):
     pieces, ys, highs, lows, parts, width = a_ref.shape
     blocks = lows * ys
-    half = parts // 2
+    half = parts // 4
     rows = pieces * highs * parts
     scale = 2.0 / rows
 
     def sent(k, part):
         return pltpu.make_async_copy(held.at[part, k], o_hbm.at[part, k], sems.at[part, k])
 
+    row = lax.broadcasted_iota(jnp.int32, (1, 2 * half, width), 1)
+    sign = jnp.where(row < half, -1.0, 1.0)
     for k in range(blocks // 2):
         lead = a_ref[:, pairs[0, k] & (Y - 1), :, pairs[0, k] >> 2].reshape(rows, width)
         trail = a_ref[:, pairs[1, k] & (Y - 1), :, pairs[1, k] >> 2].reshape(pieces * highs, parts, width)
-        wide = trail.astype(jnp.float32)
-        turned = jnp.concatenate([-wide[:, half:], wide[:, :half]], axis=1).astype(jnp.bfloat16)
+        wide = trail.astype(jnp.float32).reshape(rows // (2 * half), 2 * half, width)
+        turned = (pltpu.roll(wide, half, axis=1) * sign).astype(jnp.bfloat16)
         both = jnp.concatenate([trail.reshape(rows, width), turned.reshape(rows, width)], axis=1)
         for first in range(0, 2 * width, TILE):
             total = lax.dot_general(

time: 144 us -> 144 us (level)
  no operation moved by 1% of the time
where the time goes in v5:
time: 144 us
  blocking collectives  134 us (93%)
  Pallas kernels  9.45 us (7%)
    all_to_all x1, blocking collectives, body(): lax.all_to_all(whitened, ('pair', 'win'), split_axis=0, concat_axis=0, ti...  134 us
    pallas_call x1, Pallas kernels, products(): pl.pallas_call(products_kernel, in_specs=[pl.BlockSpec(memory_space=pltpu...  5.26 us
    pallas_call x1, Pallas kernels, whiten(): pl.pallas_call(whiten_kernel, in_specs=[hbm, hbm, hbm], out_specs=[pl.Blo...  4.18 us

profile of v5, /device:TPU:1, one launch (start us, length us, event | category | flops | bytes accessed | tf_op | source)
XLA Modules:
  0.0 143.9 jit_solution(17740072859393933840)
XLA Ops:
  0.7 4.2 %whiten.1 = (bf16[256,16,640]{2,1,0:T(8,128)(2,1)S(1)}, s32[2,4]{1,0:T(2,128)S(1)}) custom-call(s32[7,8]{1,0:T(8,128)} %plan_hbm.1, s32[1]{0:T(128)S(6)} %copy.5.round_hbm, bf16[2,8,256,640]{3,2,1,0:T(8,128)(2,1)} %x_hbm.1), custom_call_target="tpu_custom_call" | custom-call | tf_op jit(solution)/shard_map/whiten/pallas_call | solution.py:113
  4.8 133.8 %all_to_all.5 = bf16[256,16,640]{2,1,0:T(8,128)(2,1)S(1)} all-to-all(bf16[256,16,640]{2,1,0:T(8,128)(2,1)S(1)} %get-tuple-element.8), channel_id=1, replica_groups={{0,128,8,136,16,144,24,152,32,160,40,168,48,176,56,184,64,192,72,200,80..., dimensions={0} | all-to-all | bytes 10485760 | tf_op jit(solution)/shard_map/all_to_all | solution.py:200
  138.7 5.3 %products.1 = bf16[2,4,640,640]{3,2,1,0:T(8,128)(2,1)} custom-call(s32[2,4]{1,0:T(2,128)S(1)} %get-tuple-element.7.pairs, bf16[8,4,4,2,16,640]{5,4,3,2,1,0:T(8,128)(2,1)S(1)} %bitcast.4), custom_call_target="tpu_custom_call" | custom-call | tf_op jit(solution)/shard_map/products/pallas_call | solution.py:178

commit v6 on v4

--- a/solution.py
+++ b/solution.py
@@ -129,35 +129,42 @@
     rows = pieces * highs * parts
     scale = 2.0 / rows
 
-    def sent(k, part):
-        return pltpu.make_async_copy(held.at[part, k], o_hbm.at[part, k], sems.at[part, k])
-
+    def sent(k, part, top, bottom):
+        some = pl.ds(top, bottom - top)
+        return pltpu.make_async_copy(
+            held.at[part, k, some], o_hbm.at[part, k, some], sems.at[part, k, int(top > 0)]
+        )
+
+    copies = []
     for k in range(blocks // 2):
         lead = a_ref[:, pairs[0, k] & (Y - 1), :, pairs[0, k] >> 2].reshape(rows, width)
         trail = a_ref[:, pairs[1, k] & (Y - 1), :, pairs[1, k] >> 2].reshape(pieces * highs, parts, width)
         wide = trail.astype(jnp.float32)
         turned = jnp.concatenate([-wide[:, half:], wide[:, :half]], axis=1).astype(jnp.bfloat16)
         both = jnp.concatenate([trail.reshape(rows, width), turned.reshape(rows, width)], axis=1)
-        for first in range(0, 2 * width, TILE):
-            total = lax.dot_general(
-                lead,
-                both[:, first : first + TILE],
-                (((0,), (0,)), ((), ())),
-                preferred_element_type=jnp.float32,
-            )
-            result = (total * scale).astype(held.dtype)
-            last = first + result.shape[1]
-            cut = min(max(width - first, 0), result.shape[1])
-            if cut:
-                held[0, k, :, first : first + cut] = result[:, :cut]
-            if cut < result.shape[1]:
-                held[1, k, :, first + cut - width : last - width] = result[:, cut:]
-            if first < width <= last:
-                sent(k, 0).start()
-        sent(k, 1).start()
-    for k in range(blocks // 2):
-        for part in range(2):
-            sent(k, part).wait()
+        cuts = (0, width - TILE, width) if k == blocks // 2 - 1 else (0, width)
+        for top, bottom in zip(cuts[:-1], cuts[1:]):
+            for first in range(0, 2 * width, TILE):
+                total = lax.dot_general(
+                    lead[:, top:bottom],
+                    both[:, first : first + TILE],
+                    (((0,), (0,)), ((), ())),
+                    preferred_element_type=jnp.float32,
+                )
+                result = (total * scale).astype(held.dtype)
+                last = first + result.shape[1]
+                cut = min(max(width - first, 0), result.shape[1])
+                if cut:
+                    held[0, k, top:bottom, first : first + cut] = result[:, :cut]
+                if cut < result.shape[1]:
+                    held[1, k, top:bottom, first + cut - width : last - width] = result[:, cut:]
+                if first < width <= last:
+                    copies.append(sent(k, 0, top, bottom))
+                    copies[-1].start()
+            copies.append(sent(k, 1, top, bottom))
+            copies[-1].start()
+    for c in copies:
+        c.wait()
 
 
 def products(arrived, pairs):
@@ -173,7 +180,7 @@
         out_shape=jax.ShapeDtypeStruct((2, blocks // 2, width, width), jnp.bfloat16),
         scratch_shapes=[
             pltpu.VMEM((2, blocks // 2, width, width), jnp.bfloat16),
-            pltpu.SemaphoreType.DMA((2, blocks // 2)),
+            pltpu.SemaphoreType.DMA((2, blocks // 2, 2)),
         ],
         compiler_params=pltpu.CompilerParams(vmem_limit_bytes=VMEM_LIMIT),
         name="products",

time: 144 us -> 144 us (level)
  no operation moved by 1% of the time
where the time goes in v6:
time: 144 us
  blocking collectives  134 us (93%)
  Pallas kernels  9.38 us (7%)
    all_to_all x1, blocking collectives, body(): lax.all_to_all(whitened, ('pair', 'win'), split_axis=0, concat_axis=0, ti...  134 us
    pallas_call x1, Pallas kernels, products(): pl.pallas_call(products_kernel, in_specs=[pl.BlockSpec(memory_space=pltpu...  5.14 us
    pallas_call x1, Pallas kernels, whiten(): pl.pallas_call(whiten_kernel, in_specs=[hbm, hbm, hbm], out_specs=[pl.Blo...  4.24 us

profile of v6, /device:TPU:1, one launch (start us, length us, event | category | flops | bytes accessed | tf_op | source)
XLA Modules:
  0.0 143.9 jit_solution(514773200815084832)
XLA Ops:
  0.7 4.2 %whiten.1 = (bf16[256,16,640]{2,1,0:T(8,128)(2,1)S(1)}, s32[2,4]{1,0:T(2,128)S(1)}) custom-call(s32[7,8]{1,0:T(8,128)} %plan_hbm.1, s32[1]{0:T(128)S(6)} %copy.5.round_hbm, bf16[2,8,256,640]{3,2,1,0:T(8,128)(2,1)} %x_hbm.1), custom_call_target="tpu_custom_call" | custom-call | tf_op jit(solution)/shard_map/whiten/pallas_call | solution.py:104
  4.9 133.8 %all_to_all.5 = bf16[256,16,640]{2,1,0:T(8,128)(2,1)S(1)} all-to-all(bf16[256,16,640]{2,1,0:T(8,128)(2,1)S(1)} %get-tuple-element.8), channel_id=1, replica_groups={{0,128,8,136,16,144,24,152,32,160,40,168,48,176,56,184,64,192,72,200,80..., dimensions={0} | all-to-all | bytes 10485760 | tf_op jit(solution)/shard_map/all_to_all | solution.py:195
  138.7 5.1 %products.1 = bf16[2,4,640,640]{3,2,1,0:T(8,128)(2,1)} custom-call(s32[2,4]{1,0:T(2,128)S(1)} %get-tuple-element.7.pairs, bf16[8,4,4,2,16,640]{5,4,3,2,1,0:T(8,128)(2,1)S(1)} %bitcast.4), custom_call_target="tpu_custom_call" | custom-call | tf_op jit(solution)/shard_map/products/pallas_call | solution.py:173

commit v7 on v6

--- a/solution.py
+++ b/solution.py
@@ -38,7 +38,9 @@
         pairs[1, k] = rival
 
 
-def whiten_kernel(plan_hbm, round_hbm, x_hbm, o_ref, pairs, x_vmem, scale, plan, round_index, sems, small_sems):
+def whiten_kernel(
+    plan_hbm, round_hbm, x_hbm, o_ref, pairs, x_vmem, early, scale, plan, round_index, sems, small_sems
+):
     _, windows, bins, width = x_hbm.shape
 
     def copy(w):
@@ -53,7 +55,8 @@
     for w in range(windows):
         copy(w).start()
 
-    series = 2 * windows
+    half = windows // 2
+    series = 2 * half
     count = series * GROUP
     row = lax.broadcasted_iota(jnp.int32, (count, count), 0)
     column = lax.broadcasted_iota(jnp.int32, (count, count), 1)
@@ -79,21 +82,27 @@
             total = (totals[0] + totals[1]) + (totals[2] + totals[3])
             energies.append(jnp.sum(total, axis=0, keepdims=True))
         energy = jnp.concatenate(energies, axis=1) * (1.0 / bins)
-        scale[pl.ds(w, 1)] = lax.rsqrt(energy + EPS)
+        inverse = lax.rsqrt(energy + EPS)
+        side = w // half
+        for part in range(2):
+            scale[side, pl.ds(part * half + w - side * half, 1)] = inverse
         return carry
 
-    lax.fori_loop(0, windows, one_window, 0)
-    inverse = scale[...]
-
-    for first in range(0, bins, JOIN * GROUP):
-        groups = range(first, first + JOIN * GROUP, GROUP)
-        rows = [x_vmem[:, :, f : f + GROUP].reshape(count, width) for f in groups]
-        moved = jnp.dot(swap, jnp.concatenate(rows, axis=1), preferred_element_type=jnp.float32)
-        for j, f in enumerate(groups):
-            group = moved[:, j * width : (j + 1) * width].reshape(2 * GROUP, windows, width) * inverse
-            group = group.astype(o_ref.dtype).reshape(GROUP, series, width)
-            for i in range(GROUP):
-                o_ref[slot_of(f + i)] = group[i]
+    for side in range(2):
+        lax.fori_loop(side * half, (side + 1) * half, one_window, 0)
+        inverse = scale[side]
+        for first in range(0, bins, JOIN * GROUP):
+            groups = range(first, first + JOIN * GROUP, GROUP)
+            rows = [x_vmem[:, side * half : (side + 1) * half, f : f + GROUP].reshape(count, width) for f in groups]
+            moved = jnp.dot(swap, jnp.concatenate(rows, axis=1), preferred_element_type=jnp.float32)
+            for j, f in enumerate(groups):
+                group = moved[:, j * width : (j + 1) * width].reshape(GROUP, series, width) * inverse
+                if side == 0:
+                    early[f : f + GROUP] = group
+                    continue
+                group = jnp.concatenate([early[f : f + GROUP], group], axis=1).astype(o_ref.dtype)
+                for i in range(GROUP):
+                    o_ref[slot_of(f + i)] = group[i]
 
 
 def whiten(spectra, plan, round_index):
@@ -111,7 +120,8 @@
         ],
         scratch_shapes=[
             pltpu.VMEM((2, windows, bins, width), jnp.bfloat16),
-            pltpu.VMEM((windows, width), jnp.float32),
+            pltpu.VMEM((bins, windows, width), jnp.float32),
+            pltpu.VMEM((2, windows, width), jnp.float32),
             pltpu.SMEM(plan.shape, jnp.int32),
             pltpu.SMEM(round_index.shape, jnp.int32),
             pltpu.SemaphoreType.DMA((windows,)),
@@ -125,7 +135,7 @@
 def products_kernel(pairs, a_ref, o_hbm, held, sems):
     pieces, ys, highs, lows, parts, width = a_ref.shape
     blocks = lows * ys
-    half = parts // 2
+    half = parts // 4
     rows = pieces * highs * parts
     scale = 2.0 / rows
 
@@ -136,11 +146,13 @@
         )
 
     copies = []
+    row = lax.broadcasted_iota(jnp.int32, (1, 2 * half, width), 1)
+    sign = jnp.where(row < half, -1.0, 1.0)
     for k in range(blocks // 2):
         lead = a_ref[:, pairs[0, k] & (Y - 1), :, pairs[0, k] >> 2].reshape(rows, width)
         trail = a_ref[:, pairs[1, k] & (Y - 1), :, pairs[1, k] >> 2].reshape(pieces * highs, parts, width)
-        wide = trail.astype(jnp.float32)
-        turned = jnp.concatenate([-wide[:, half:], wide[:, :half]], axis=1).astype(jnp.bfloat16)
+        wide = trail.astype(jnp.float32).reshape(rows // (2 * half), 2 * half, width)
+        turned = (pltpu.roll(wide, half, axis=1) * sign).astype(jnp.bfloat16)
         both = jnp.concatenate([trail.reshape(rows, width), turned.reshape(rows, width)], axis=1)
         cuts = (0, width - TILE, width) if k == blocks // 2 - 1 else (0, width)
         for top, bottom in zip(cuts[:-1], cuts[1:]):

time: 144 us -> 144 us (level)
  no operation moved by 1% of the time
where the time goes in v7:
time: 144 us
  blocking collectives  134 us (93%)
  Pallas kernels  9.34 us (6%)
    all_to_all x1, blocking collectives, body(): lax.all_to_all(whitened, ('pair', 'win'), split_axis=0, concat_axis=0, ti...  134 us
    pallas_call x1, Pallas kernels, products(): pl.pallas_call(products_kernel, in_specs=[pl.BlockSpec(memory_space=pltpu...  5.16 us
    pallas_call x1, Pallas kernels, whiten(): pl.pallas_call(whiten_kernel, in_specs=[hbm, hbm, hbm], out_specs=[pl.Blo...  4.18 us

profile of v7, /device:TPU:1, one launch (start us, length us, event | category | flops | bytes accessed | tf_op | source)
XLA Modules:
  0.0 143.8 jit_solution(11502286331147280638)
XLA Ops:
  0.7 4.2 %whiten.1 = (bf16[256,16,640]{2,1,0:T(8,128)(2,1)S(1)}, s32[2,4]{1,0:T(2,128)S(1)}) custom-call(s32[7,8]{1,0:T(8,128)} %plan_hbm.1, s32[1]{0:T(128)S(6)} %copy.5.round_hbm, bf16[2,8,256,640]{3,2,1,0:T(8,128)(2,1)} %x_hbm.1), custom_call_target="tpu_custom_call" | custom-call | tf_op jit(solution)/shard_map/whiten/pallas_call | solution.py:113
  4.8 133.8 %all_to_all.5 = bf16[256,16,640]{2,1,0:T(8,128)(2,1)S(1)} all-to-all(bf16[256,16,640]{2,1,0:T(8,128)(2,1)S(1)} %get-tuple-element.8), channel_id=1, replica_groups={{0,128,8,136,16,144,24,152,32,160,40,168,48,176,56,184,64,192,72,200,80..., dimensions={0} | all-to-all | bytes 10485760 | tf_op jit(solution)/shard_map/all_to_all | solution.py:207
  138.7 5.2 %products.1 = bf16[2,4,640,640]{3,2,1,0:T(8,128)(2,1)} custom-call(s32[2,4]{1,0:T(2,128)S(1)} %get-tuple-element.7.pairs, bf16[8,4,4,2,16,640]{5,4,3,2,1,0:T(8,128)(2,1)S(1)} %bitcast.4), custom_call_target="tpu_custom_call" | custom-call | tf_op jit(solution)/shard_map/products/pallas_call | solution.py:185

commit v8 on v7

--- a/solution.py
+++ b/solution.py
@@ -10,7 +10,7 @@
 ROWS = 32
 GROUP = 16
 TILE = 256
-JOIN = 2
+JOIN = 4
 Z, Y, X, C = 8, 4, 4, 2
 VMEM_LIMIT = 24 * 1024 * 1024
 

time: 144 us -> 144 us (level)
  no operation moved by 1% of the time
where the time goes in v8:
time: 144 us
  blocking collectives  134 us (93%)
  Pallas kernels  9.35 us (6%)
    all_to_all x1, blocking collectives, body(): lax.all_to_all(whitened, ('pair', 'win'), split_axis=0, concat_axis=0, ti...  134 us
    pallas_call x1, Pallas kernels, products(): pl.pallas_call(products_kernel, in_specs=[pl.BlockSpec(memory_space=pltpu...  5.16 us
    pallas_call x1, Pallas kernels, whiten(): pl.pallas_call(whiten_kernel, in_specs=[hbm, hbm, hbm], out_specs=[pl.Blo...  4.19 us

profile of v8, /device:TPU:1, one launch (start us, length us, event | category | flops | bytes accessed | tf_op | source)
XLA Modules:
  0.0 143.8 jit_solution(14000173861966121084)
XLA Ops:
  0.7 4.2 %whiten.1 = (bf16[256,16,640]{2,1,0:T(8,128)(2,1)S(1)}, s32[2,4]{1,0:T(2,128)S(1)}) custom-call(s32[7,8]{1,0:T(8,128)} %plan_hbm.1, s32[1]{0:T(128)S(6)} %copy.5.round_hbm, bf16[2,8,256,640]{3,2,1,0:T(8,128)(2,1)} %x_hbm.1), custom_call_target="tpu_custom_call" | custom-call | tf_op jit(solution)/shard_map/whiten/pallas_call | solution.py:113
  4.8 133.8 %all_to_all.5 = bf16[256,16,640]{2,1,0:T(8,128)(2,1)S(1)} all-to-all(bf16[256,16,640]{2,1,0:T(8,128)(2,1)S(1)} %get-tuple-element.8), channel_id=1, replica_groups={{0,128,8,136,16,144,24,152,32,160,40,168,48,176,56,184,64,192,72,200,80..., dimensions={0} | all-to-all | bytes 10485760 | tf_op jit(solution)/shard_map/all_to_all | solution.py:207
  138.7 5.2 %products.1 = bf16[2,4,640,640]{3,2,1,0:T(8,128)(2,1)} custom-call(s32[2,4]{1,0:T(2,128)S(1)} %get-tuple-element.7.pairs, bf16[8,4,4,2,16,640]{5,4,3,2,1,0:T(8,128)(2,1)S(1)} %bitcast.4), custom_call_target="tpu_custom_call" | custom-call | tf_op jit(solution)/shard_map/products/pallas_call | solution.py:185
